TPU v7x, 32 devices: a whole 2x2x4 slice. The times are simulated.
32 devices in a mesh: seq: 8 (over y, x, core), dp: 4 (over z).
Axes of the slice: x: 2, y: 2, z: 4, core: 2. Of those that a mesh axis runs over, the one named last changes fastest.
Arguments:
- coarse: bfloat16 [4, 2048, 768], P('dp', 'seq'), may hold values from -6 to 6
- skip: bfloat16 [4, 4096, 768], P('dp', 'seq'), may hold values from -6 to 6
- skip_weight: bfloat16 [768, 768], P('seq'), may hold values from -0.21875 to 0.21875
- depth_taps: float32 [3, 768], replicated, may hold values from -3 to 3
- cotangent: bfloat16 [4, 4096, 768], P('dp', 'seq'), may hold values from -6 to 6
Outputs:
- grad_coarse: bfloat16 [4, 2048, 768], P('dp', 'seq')
- grad_skip: bfloat16 [4, 4096, 768], P('dp', 'seq')
- grad_skip_weight: float32 [768, 768], P('seq')
- grad_taps: float32 [3, 768], replicated
All inputs are finite; a program needn't handle non-finite values.
Results may differ from a plain program's by a relative error of at most 0.006.
Values may be sent and summed in bfloat16 or wider, within the bound.
A program may use at most 64 MiB of HBM per device.

v0:
```python
import math

import jax
import jax.numpy as jnp
from jax import lax
from jax.sharding import PartitionSpec as P

inv_root_two = 0.7071067811865476
inv_root_tau = 0.3989422804014327


def padded_2(cells, sides, width):
    for axis, dim in sides:
        count = lax.axis_size(axis)
        ends = count - 1
        head = lax.slice_in_dim(cells, 0, width, axis=dim)
        tail = lax.slice_in_dim(cells, cells.shape[dim] - width, cells.shape[dim], axis=dim)
        cells = jnp.concatenate(
            [
                lax.ppermute(tail, axis, [(i, (i + 1) % count) for i in range(ends)]),
                cells,
                lax.ppermute(head, axis, [((i + 1) % count, i) for i in range(ends)]),
            ],
            axis=dim,
        )
    return cells


def gelu_slope(pre_act):
    normal_cdf = 0.5 * (1.0 + lax.erf(pre_act * inv_root_two))
    normal_pdf = jnp.exp(-0.5 * pre_act * pre_act) * inv_root_tau
    return normal_cdf + pre_act * normal_pdf


def local(coarse, skip, skip_weight, depth_taps, cotangent):
    batch_rows, fine_rows, channels = skip.shape
    flat_count = batch_rows * fine_rows
    shard_rows = skip_weight.shape[0]
    flat_skip = skip.reshape(flat_count, channels)
    full_weight = lax.all_gather(skip_weight, "seq", axis=0, tiled=True)
    projected = jnp.dot(flat_skip, full_weight, preferred_element_type=jnp.float32)
    upsampled = jnp.broadcast_to(
        coarse[:, :, None, :], (batch_rows, fine_rows // 2, 2, channels)
    ).reshape(flat_count, channels)
    merged = (
        (upsampled.astype(jnp.float32) + projected)
        .astype(jnp.bfloat16)
        .reshape(batch_rows, fine_rows, channels)
    )
    padded = padded_2(merged, (("seq", 1),), 1)
    pre_act = (
        depth_taps[0] * padded[:, :-2]
        + depth_taps[1] * padded[:, 1:-1]
        + depth_taps[2] * padded[:, 2:]
    )
    grad_pre = (cotangent * gelu_slope(pre_act)).astype(jnp.bfloat16)
    grad_padded = padded_2(grad_pre, (("seq", 1),), 1)
    grad_merged = (
        cotangent.astype(jnp.float32)
        + depth_taps[0] * grad_padded[:, 2:]
        + depth_taps[1] * grad_padded[:, 1:-1]
        + depth_taps[2] * grad_padded[:, :-2]
    ).astype(jnp.bfloat16)
    flat_grad = grad_merged.reshape(flat_count, channels)
    grad_wide = grad_pre.astype(jnp.float32)
    tap_terms = jnp.stack(
        [
            jnp.sum(
                padded[:, offset : offset + fine_rows].astype(jnp.float32) * grad_wide, axis=(0, 1)
            )
            for offset in range(3)
        ]
    )
    grad_scale = 1.0 / math.sqrt(flat_count * lax.axis_size("seq") * lax.axis_size("dp"))
    summed, tap_sum = lax.psum(
        (
            lax.dot_general(
                flat_skip, flat_grad, (((0,), (0,)), ((), ())), preferred_element_type=jnp.float32
            ),
            tap_terms,
        ),
        ("seq", "dp"),
    )
    weight_sum = lax.dynamic_slice_in_dim(summed, lax.axis_index("seq") * shard_rows, shard_rows, 0)
    grad_skip = lax.dot_general(
        flat_grad, full_weight, (((1,), (1,)), ((), ())), preferred_element_type=jnp.float32
    )
    grad_coarse = (
        grad_merged.astype(jnp.float32)
        .reshape(batch_rows, fine_rows // 2, 2, channels)
        .sum(axis=2)
        .astype(jnp.bfloat16)
    )
    grad_skip = grad_skip.astype(jnp.bfloat16).reshape(batch_rows, fine_rows, channels)
    return (grad_coarse, grad_skip, weight_sum * grad_scale, tap_sum * grad_scale)


def solution(mesh):
    placed = (P("dp", "seq", None), P("dp", "seq", None), P("seq", None), P(), P("dp", "seq", None))
    return jax.shard_map(
        local,
        mesh=mesh,
        in_specs=placed,
        out_specs=(P("dp", "seq", None), P("dp", "seq", None), P("seq", None), P()),
        check_vma=False,
    )
```

profile of v0, /device:TPU:0, one launch (start us, length us, event | category | flops | bytes accessed | tf_op | source)
XLA Modules:
  0.0 205.3 jit_solution(4860683564422918321)
XLA Ops:
  7.2 0.0 copy-start
  7.2 0.0 all-gather.2.cloned.1.call-start
  7.2 0.7 all-gather.2.cloned.1.call-update
  7.9 0.0 all-reduce.2.cloned.1.call-start
  8.0 1.0 bitcast_convert_fusion
  9.0 0.5 broadcast_in_dim.2
  9.6 2.2 %convert_element_type.69 = f32[512,768]{1,0:T(8,128)} reshape(f32[256,2,768]{2,1,0:T(2,128)S(1)} %broadcast_in_dim.2) | data formatting | bytes 3145728 | tf_op jit(solution)/shard_map/convert_element_type | solution.py:46
  11.8 0.0 copy-start.2
  11.8 0.0 copy-start.1
  11.8 24.9 %all-gather.2.cloned.1.call-done = bf16[768,768]{1,0:T(8,128)(2,1)} async-done(((bf16[96,768]{1,0:T(8,128)(2,1)}), bf16[768,768]{1,0:T(8,128)(2,1)}) %all-gather.2.cloned.1.call-update) | async-done | bytes 1179664 | tf_op jit(solution)/shard_map/all_gather | solution.py:40
  36.7 0.0 copy-done
  36.7 2.5 %add_convert_fusion = bf16[512,768]{1,0:T(8,128)(2,1)S(1)} fusion(f32[512,768]{1,0:T(8,128)} %convert_element_type.69, bf16[768,768]{1,0:T(8,128)(2,1)} %all-gather.2.cloned.1.call-done, bf16[1,512,768]{2,1,0:T(8,128)(2,1)S(1)} %copy-done), kind=kOutput, calls=%fused_computation.26 | convolution fusion | flops 604766208 | bytes 4325376 | tf_op jit(solution)/shard_map/dot_general | solution.py:41
  39.3 2.2 %collective-permute-start = (bf16[1,1,768]{2,1,0:T(2,128)(2,1)S(1)}, bf16[1,1,768]{2,1,0:T(2,128)(2,1)S(1)}, u32[]{:S(2)}, u32[]{:S(2)}) collective-permute-start(bf16[1,1,768]{2,1,0:T(2,128)(2,1)S(1)} %get-tuple-element.18), channel_id=1, source_target_pairs={{0,4},{4,8},{8,12},{12,16},{16,20},{20,24},{24,28},{1,5},{5,9},{9,... | collective-permute-start | bytes 4616 | tf_op jit(solution)/shard_map/ppermute | solution.py:20
  41.5 1.3 collective-permute-start.1
  42.8 0.0 copy-done.2
  42.8 0.0 collective-permute-done
  42.8 2.5 %collective-permute-done.1 = bf16[1,1,768]{2,1,0:T(2,128)(2,1)S(1)} collective-permute-done((bf16[1,1,768]{2,1,0:T(2,128)(2,1)S(1)}, bf16[1,1,768]{2,1,0:T(2,128)(2,1)S(1)}, u32[]{:S(2)}, u32[]{:S(2)}) %collective-permute-start.1) | collective-permute-done | bytes 1568 | tf_op jit(solution)/shard_map/ppermute | solution.py:22
  45.3 0.0 copy-done.1
  45.3 1.8 fusion.11
  47.1 4.3 %collective-permute-start.3 = (bf16[1,1,768]{2,1,0:T(2,128)(2,1)S(1)}, bf16[1,1,768]{2,1,0:T(2,128)(2,1)S(1)}, u32[]{:S(2)}, u32[]{:S(2)}) collective-permute-start(bf16[1,1,768]{2,1,0:T(2,128)(2,1)S(1)} %get-tuple-element.16), channel_id=1, source_target_pairs={{0,4},{4,8},{8,12},{12,16},{16,20},{20,24},{24,28},{1,5},{5,9},{9,... | collective-permute-start | bytes 4616 | tf_op jit(solution)/shard_map/ppermute | solution.py:20
  51.4 1.3 collective-permute-start.2
  52.7 0.0 collective-permute-done.3
  52.7 1.7 collective-permute-done.2
  54.4 0.7 fusion.3
  55.1 2.2 %convolution_bitcast_fusion = f32[768,768]{0,1:T(8,128)} fusion(bf16[1,512,768]{2,1,0:T(8,128)(2,1)S(1)} %fusion.3, bf16[1,512,768]{2,1,0:T(8,128)(2,1)S(1)} %copy-done), kind=kOutput, calls=%fused_computation.11 | convolution fusion | flops 603979776 | bytes 3932160 | tf_op jit(solution)/shard_map/dot_general | solution.py:77
  57.3 0.0 all-reduce.2.cloned.1.call-update
  57.3 0.0 copy-start.3
  57.4 43.0 %psum.15 = f32[3,768]{1,0:T(4,128)S(1)} all-reduce(f32[3,768]{1,0:T(4,128)S(1)} %pad_maximum_fusion.4), channel_id=1, replica_groups=mesh['seq'=8,'dp'=4] {'seq','dp'}, use_global_device_ids=true, to_apply=%region_5.0 | all-reduce | flops 2304 | bytes 18432 | tf_op jit(solution)/shard_map/psum | solution.py:75
  100.4 0.6 broadcast_multiply_fusion
  101.0 0.3 reshape.57
  101.3 2.9 %reduce.1 = bf16[256,768]{1,0:T(8,128)(2,1)} reduce(bf16[256,2,768]{2,1,0:T(2,128)(2,1)S(1)} %reshape.57, bf16[]{:T(256)} %constant.30), dimensions={1}, to_apply=%region_0.0.clone | reduce | flops 196608 | bytes 1179650 | tf_op jit(solution)/shard_map/reduce_sum | solution.py:91
  104.2 0.0 copy-done.3
  104.2 1.7 fusion.14
  105.9 90.4 %all-reduce.2.cloned.1.call-done = f32[768,768]{0,1:T(8,128)} async-done(((f32[768,768]{0,1:T(8,128)}), f32[768,768]{0,1:T(8,128)}) %all-reduce.2.cloned.1.call-update) | async-done | bytes 2359312 | tf_op jit(solution)/shard_map/psum | solution.py:75
  196.3 1.3 dynamic-slice_multiply_fusion
  197.6 0.9 copy.9
  (7 shorter events, 0.1 us)
Async XLA Ops:
  7.2 29.5 %copy-start = (bf16[1,512,768]{2,1,0:T(8,128)(2,1)S(1)}, bf16[1,512,768]{2,1,0:T(8,128)(2,1)}, u32[]{:S(2)}) copy-start(bf16[1,512,768]{2,1,0:T(8,128)(2,1)} %param.6) | copy-start | bytes 2359300
  7.2 29.5 %all-gather.2.cloned.1.call-start = ((), (), s32[]{:S(2)}) async-start(), calls=%async_computation | async-start | bytes 1327104 | tf_op jit(solution)/shard_map/all_gather | solution.py:40
  7.9 188.4 %all-reduce.2.cloned.1.call-start = ((), (), s32[]{:S(2)}) async-start(), calls=%async_computation.1 | async-start | bytes 4718592 | tf_op jit(solution)/shard_map/psum | solution.py:75
  11.8 31.0 %copy-start.2 = (f32[3,768]{1,0:T(4,128)S(1)}, f32[3,768]{1,0:T(4,128)}, u32[]{:S(2)}) copy-start(f32[3,768]{1,0:T(4,128)} %param.8) | copy-start | bytes 27652
  11.8 33.5 %copy-start.1 = (bf16[1,512,768]{2,1,0:T(8,128)(2,1)S(1)}, bf16[1,512,768]{2,1,0:T(8,128)(2,1)}, u32[]{:S(2)}) copy-start(bf16[1,512,768]{2,1,0:T(8,128)(2,1)} %param.9) | copy-start | bytes 2359300
  39.3 3.5 %collective-permute-start = (bf16[1,1,768]{2,1,0:T(2,128)(2,1)S(1)}, bf16[1,1,768]{2,1,0:T(2,128)(2,1)S(1)}, u32[]{:S(2)}, u32[]{:S(2)}) collective-permute-start(bf16[1,1,768]{2,1,0:T(2,128)(2,1)S(1)} %get-tuple-element.18), channel_id=1, source_target_pairs={{0,4},{4,8},{8,12},{12,16},{16,20},{20,24},{24,28},{1,5},{5,9},{9,... | collective-permute-start | bytes 4616 | tf_op jit(solution)/shard_map/ppermute | solution.py:20
  41.5 3.9 %collective-permute-start.1 = (bf16[1,1,768]{2,1,0:T(2,128)(2,1)S(1)}, bf16[1,1,768]{2,1,0:T(2,128)(2,1)S(1)}, u32[]{:S(2)}, u32[]{:S(2)}) collective-permute-start(bf16[1,1,768]{2,1,0:T(2,128)(2,1)S(1)} %get-tuple-element.17), channel_id=1, source_target_pairs={{4,0},{8,4},{12,8},{16,12},{20,16},{24,20},{28,24},{5,1},{9,5},{13... | collective-permute-start | bytes 4616 | tf_op jit(solution)/shard_map/ppermute | solution.py:22
  47.1 5.6 %collective-permute-start.3 = (bf16[1,1,768]{2,1,0:T(2,128)(2,1)S(1)}, bf16[1,1,768]{2,1,0:T(2,128)(2,1)S(1)}, u32[]{:S(2)}, u32[]{:S(2)}) collective-permute-start(bf16[1,1,768]{2,1,0:T(2,128)(2,1)S(1)} %get-tuple-element.16), channel_id=1, source_target_pairs={{0,4},{4,8},{8,12},{12,16},{16,20},{20,24},{24,28},{1,5},{5,9},{9,... | collective-permute-start | bytes 4616 | tf_op jit(solution)/shard_map/ppermute | solution.py:20
  51.4 3.1 %collective-permute-start.2 = (bf16[1,1,768]{2,1,0:T(2,128)(2,1)S(1)}, bf16[1,1,768]{2,1,0:T(2,128)(2,1)S(1)}, u32[]{:S(2)}, u32[]{:S(2)}) collective-permute-start(bf16[1,1,768]{2,1,0:T(2,128)(2,1)S(1)} %get-tuple-element.15), channel_id=1, source_target_pairs={{4,0},{8,4},{12,8},{16,12},{20,16},{24,20},{28,24},{5,1},{9,5},{13... | collective-permute-start | bytes 4616 | tf_op jit(solution)/shard_map/ppermute | solution.py:22
  57.3 46.9 %copy-start.3 = (bf16[768,768]{1,0:T(8,128)(2,1)S(1)}, bf16[768,768]{1,0:T(8,128)(2,1)}, u32[]{:S(2)}) copy-start(bf16[768,768]{1,0:T(8,128)(2,1)} %all-gather.2.cloned.1.call-done) | copy-start | bytes 3538948
Sparse Core Ops, SparseCore 0:
  9.9 26.7 all-gather.1
  57.5 138.7 all-reduce.1
where the time goes:
time: 206 us; the launch traced here: 205 us
  waiting for transfers between devices  120 us (58%)
  blocking collectives  43 us (21%)
  between operations  14.2 us (7%)
  starting transfers between devices  9.1 us (4%)
  other arithmetic  8.28 us (4%)
  matrix products  6.45 us (3%)
  local copies, waits for them, and re-layouts  4.03 us (2%)
    psum x1, waiting for transfers between devices, local(): lax.psum((lax.dot_general(flat_skip, flat_grad, (((0,), (0,)), ((), ())),...  90.4 us
    psum x1, blocking collectives, local(): lax.psum((lax.dot_general(flat_skip, flat_grad, (((0,), (0,)), ((), ())),...  43 us
    all_gather x1, waiting for transfers between devices, local(): full_weight = lax.all_gather(skip_weight, 'seq', axis=0, tiled=True)  24.9 us
    ppermute x2, starting transfers between devices, padded_2(): lax.ppermute(tail, axis, [(i, (i + 1) % count) for i in range(ends)])  6.44 us
    ppermute x2, waiting for transfers between devices, padded_2(): lax.ppermute(head, axis, [((i + 1) % count, i) for i in range(ends)])  4.26 us
  transfers between devices with their start and end apart: 6, of which 4 were waited for; matrix products, arithmetic and copies ran while one was open for 5% of the time, Pallas kernels for 0%

commit v1 on v0

--- a/solution.py
+++ b/solution.py
@@ -1,8 +1,11 @@
+import functools
 import math
 
 import jax
 import jax.numpy as jnp
 from jax import lax
+from jax.experimental import pallas as pl
+from jax.experimental.pallas import tpu as pltpu
 from jax.sharding import PartitionSpec as P
 
 inv_root_two = 0.7071067811865476
@@ -95,10 +98,566 @@
     return (grad_coarse, grad_skip, weight_sum * grad_scale, tap_sum * grad_scale)
 
 
+MESH = pl.DeviceIdType.MESH
+halo = 16
+tile = 64
+width = 256
+
+
+def send(src, dst, send_sem, recv_sem, axis, target):
+    return pltpu.make_async_remote_copy(
+        src_ref=src,
+        dst_ref=dst,
+        send_sem=send_sem,
+        recv_sem=recv_sem,
+        device_id={axis: target},
+        device_id_type=MESH,
+    )
+
+
+def kernel(
+    seq_count,
+    dp_count,
+    grad_scale,
+    coarse_hbm,
+    skip_hbm,
+    weight_ref,
+    taps_ref,
+    cot_hbm,
+    coarse_out,
+    skip_out,
+    weight_out,
+    taps_out,
+    skip_ext,
+    cot_ext,
+    coarse_ext,
+    skip_turned,
+    repeat_mat,
+    pair_mat,
+    weights,
+    merged,
+    grad_pre,
+    grad_merged,
+    coarse_grad,
+    skip_grad,
+    term_wide,
+    term_half,
+    from_core,
+    chip_half,
+    chip_own,
+    from_chips,
+    plane_wide,
+    plane_half,
+    from_planes,
+    final,
+    tap_own,
+    tap_core,
+    tap_chips,
+    tap_planes,
+    local_sem,
+    halo_send,
+    halo_recv,
+    gather_send,
+    gather_recv,
+    forward_send,
+    forward_recv,
+    sib_send,
+    sib_recv,
+    core_send,
+    core_recv,
+    chip_send,
+    chip_recv,
+    plane_send,
+    plane_recv,
+    final_send,
+    final_recv,
+    tap_send,
+    tap_recv,
+):
+    rows = skip_hbm.shape[1]
+    channels = skip_hbm.shape[2]
+    shard = weight_ref.shape[0]
+    chunks = channels // width
+    chips = seq_count // 2
+    me = lax.axis_index("seq")
+    plane = lax.axis_index("dp")
+    core = lax.rem(me, 2)
+    chip = lax.div(me, 2)
+    sibling = me + 1 - 2 * core
+    right = lax.rem(me + 1, seq_count)
+    left = lax.rem(me + seq_count - 1, seq_count)
+
+    loads = [
+        pltpu.make_async_copy(skip_hbm.at[0], skip_ext.at[pl.ds(halo, rows)], local_sem.at[0]),
+        pltpu.make_async_copy(cot_hbm.at[0], cot_ext.at[pl.ds(halo, rows)], local_sem.at[1]),
+        pltpu.make_async_copy(
+            coarse_hbm.at[0], coarse_ext.at[pl.ds(halo, rows // 2)], local_sem.at[2]
+        ),
+    ]
+    for copy in loads:
+        copy.start()
+
+    barrier = pltpu.get_barrier_semaphore()
+    for step in range(1, seq_count):
+        pl.semaphore_signal(
+            barrier, inc=1, device_id={"seq": lax.rem(me + step, seq_count)}, device_id_type=MESH
+        )
+    for step in range(1, dp_count):
+        pl.semaphore_signal(
+            barrier, inc=1, device_id={"dp": lax.rem(plane + step, dp_count)}, device_id_type=MESH
+        )
+    pl.semaphore_wait(barrier, seq_count + dp_count - 2)
+
+    sends = []
+
+    def launch(copy):
+        copy.start()
+        sends.append(copy)
+        return copy
+
+    def cols(chunk):
+        return pl.ds(chunk * width, width)
+
+    gathers, own_halves = {}, {}
+
+    def gather(chunk):
+        for step in range(1, chips):
+            target = 2 * lax.rem(chip + step, chips) + core
+            gathers[chunk, step] = launch(
+                send(
+                    weight_ref.at[:, cols(chunk)],
+                    weights.at[chunk, me],
+                    gather_send.at[chunk, step - 1],
+                    gather_recv.at[chunk, step - 1],
+                    "seq",
+                    target,
+                )
+            )
+        own_halves[chunk] = launch(
+            send(
+                weight_ref.at[:, cols(chunk)],
+                weights.at[chunk, me],
+                sib_send.at[chunk],
+                sib_recv.at[chunk],
+                "seq",
+                sibling,
+            )
+        )
+
+    gather(0)
+    halos = []
+    pairs = ((skip_hbm, skip_ext, rows), (coarse_hbm, coarse_ext, rows // 2), (cot_hbm, cot_ext, rows))
+    for number, (source, target, count) in enumerate(pairs):
+        halos.append(
+            launch(
+                send(
+                    source.at[0, pl.ds(count - halo, halo)],
+                    target.at[pl.ds(0, halo)],
+                    halo_send.at[2 * number],
+                    halo_recv.at[2 * number],
+                    "seq",
+                    right,
+                )
+            )
+        )
+        halos.append(
+            launch(
+                send(
+                    source.at[0, pl.ds(0, halo)],
+                    target.at[pl.ds(count + halo, halo)],
+                    halo_send.at[2 * number + 1],
+                    halo_recv.at[2 * number + 1],
+                    "seq",
+                    left,
+                )
+            )
+        )
+    for chunk in range(1, chunks):
+        gather(chunk)
+
+    for chunk in range(chunks):
+        weights[chunk, me] = weight_ref[:, cols(chunk)]
+    out_row = lax.broadcasted_iota(jnp.int32, repeat_mat.shape, 0)
+    in_row = lax.broadcasted_iota(jnp.int32, repeat_mat.shape, 1)
+    repeat_mat[...] = jnp.where(
+        lax.shift_right_logical(out_row, 1) + halo // 2 == in_row, 1.0, 0.0
+    ).astype(jnp.bfloat16)
+    out_row = lax.broadcasted_iota(jnp.int32, pair_mat.shape, 0)
+    in_row = lax.broadcasted_iota(jnp.int32, pair_mat.shape, 1)
+    pair_mat[...] = jnp.where(lax.shift_right_logical(in_row, 1) == out_row, 1.0, 0.0).astype(
+        jnp.bfloat16
+    )
+    tap_own[...] = jnp.zeros_like(tap_own)
+    for copy in loads:
+        copy.wait()
+    skip_turned[...] = skip_ext[pl.ds(halo, rows), :].T
+
+    low_in = jnp.where(me == 0, 0.0, 1.0)
+    high_in = jnp.where(me == seq_count - 1, 0.0, 1.0)
+    forwards = {}
+
+    def forward(chunk):
+        for step in range(1, chips):
+            gathers[chunk, step].wait_recv()
+            owner = 2 * lax.rem(chip + chips - step, chips) + core
+            forwards[chunk, step] = launch(
+                send(
+                    weights.at[chunk, owner],
+                    weights.at[chunk, owner],
+                    forward_send.at[chunk, step - 1],
+                    forward_recv.at[chunk, step - 1],
+                    "seq",
+                    sibling,
+                )
+            )
+
+    def project(chunk):
+        own_halves[chunk].wait_recv()
+        for step in range(1, chips):
+            forwards[chunk, step].wait_recv()
+        dense = weights[chunk].reshape(channels, width)
+        values = jnp.dot(skip_ext[...], dense, preferred_element_type=jnp.float32) + jnp.dot(
+            repeat_mat[...], coarse_ext[:, cols(chunk)], preferred_element_type=jnp.float32
+        )
+        values = values.astype(jnp.bfloat16).astype(jnp.float32)
+        merged[pl.ds(0, halo), :] = values[:halo] * low_in
+        merged[pl.ds(halo, rows), :] = values[halo : halo + rows]
+        merged[pl.ds(halo + rows, halo), :] = values[halo + rows :] * high_in
+
+    def slopes(chunk):
+        tap = [taps_ref[pl.ds(k, 1), cols(chunk)] for k in range(3)]
+
+        def one(first, count, cot):
+            near = [merged[pl.ds(first + k - 1, count), :] for k in range(3)]
+            pre_act = tap[0] * near[0] + tap[1] * near[1] + tap[2] * near[2]
+            return near, (cot * gelu_slope(pre_act)).astype(jnp.bfloat16).astype(jnp.float32)
+
+        edge = cot_ext[pl.ds(0, halo), cols(chunk)].astype(jnp.float32)
+        grad_pre[pl.ds(8, 8), :] = one(8, 8, edge[8:])[1] * low_in
+        edge = cot_ext[pl.ds(halo + rows, halo), cols(chunk)].astype(jnp.float32)
+        grad_pre[pl.ds(halo + rows, 8), :] = one(halo + rows, 8, edge[:8])[1] * high_in
+
+        def body(number, totals):
+            first = halo + number * tile
+            cot = cot_ext[pl.ds(first, tile), cols(chunk)].astype(jnp.float32)
+            near, grad = one(first, tile, cot)
+            grad_pre[pl.ds(first, tile), :] = grad
+            return tuple(
+                total + jnp.sum((part * grad).reshape(tile // 8, 8, width), axis=0)
+                for total, part in zip(totals, near)
+            )
+
+        zero = jnp.zeros((8, width), jnp.float32)
+        totals = (zero, zero, zero)
+        for number in range(rows // tile):
+            totals = body(number, totals)
+        for k in range(3):
+            tap_own[pl.ds(k, 1), cols(chunk)] = jnp.sum(totals[k], axis=0, keepdims=True)
+
+    def back(chunk):
+        tap = [taps_ref[pl.ds(k, 1), cols(chunk)] for k in range(3)]
+
+        for number in range(rows // tile):
+            first = halo + number * tile
+            cot = cot_ext[pl.ds(first, tile), cols(chunk)].astype(jnp.float32)
+            grad_merged[pl.ds(first - halo, tile), cols(chunk)] = (
+                cot
+                + tap[0] * grad_pre[pl.ds(first + 1, tile), :]
+                + tap[1] * grad_pre[pl.ds(first, tile), :]
+                + tap[2] * grad_pre[pl.ds(first - 1, tile), :]
+            ).astype(jnp.bfloat16)
+
+    core_copies, chip_copies, plane_copies, final_copies = {}, {}, {}, {}
+
+    def weight_terms(chunk):
+        terms = jnp.dot(
+            skip_turned[...], grad_merged[:, cols(chunk)], preferred_element_type=jnp.float32
+        )
+        for block in range(seq_count):
+            part = terms[block * shard : (block + 1) * shard]
+            term_wide[chunk, block % 2, block // 2] = part
+            term_half[chunk, block % 2, block // 2] = part.astype(jnp.bfloat16)
+        core_copies[chunk] = launch(
+            send(
+                term_half.at[chunk, 1 - core],
+                from_core.at[chunk],
+                core_send.at[chunk],
+                core_recv.at[chunk],
+                "seq",
+                sibling,
+            )
+        )
+
+    def over_chips(chunk):
+        core_copies[chunk].wait_recv()
+        for block in range(chips):
+            chip_half[chunk, block] = (
+                term_wide[chunk, core, block] + from_core[chunk, block].astype(jnp.float32)
+            ).astype(jnp.bfloat16)
+        for step in range(1, chips):
+            target = lax.rem(chip + step, chips)
+            chip_copies[chunk, step] = launch(
+                send(
+                    chip_half.at[chunk, target],
+                    from_chips.at[chunk, step - 1],
+                    chip_send.at[chunk, step - 1],
+                    chip_recv.at[chunk, step - 1],
+                    "seq",
+                    2 * target + core,
+                )
+            )
+        chip_own[chunk] = term_wide[chunk, core, chip] + from_core[chunk, chip].astype(jnp.float32)
+
+    def over_planes(chunk):
+        total = chip_own[chunk]
+        for step in range(1, chips):
+            chip_copies[chunk, step].wait_recv()
+            total = total + from_chips[chunk, step - 1].astype(jnp.float32)
+        for part in range(4):
+            piece = total[
+                (part // 2) * (shard // 2) : (part // 2 + 1) * (shard // 2),
+                (part % 2) * 128 : (part % 2 + 1) * 128,
+            ]
+            plane_wide[chunk, part] = piece
+            plane_half[chunk, part] = piece.astype(jnp.bfloat16)
+        for step in range(1, dp_count):
+            target = lax.rem(plane + step, dp_count)
+            plane_copies[chunk, step] = launch(
+                send(
+                    plane_half.at[chunk, target],
+                    from_planes.at[chunk, step - 1],
+                    plane_send.at[chunk, step - 1],
+                    plane_recv.at[chunk, step - 1],
+                    "dp",
+                    target,
+                )
+            )
+
+    def spread(chunk):
+        total = plane_wide[chunk, plane]
+        for step in range(1, dp_count):
+            plane_copies[chunk, step].wait_recv()
+            total = total + from_planes[chunk, step - 1].astype(jnp.float32)
+        final[chunk, plane] = total.astype(jnp.bfloat16)
+        for step in range(1, dp_count):
+            target = lax.rem(plane + step, dp_count)
+            final_copies[chunk, step] = launch(
+                send(
+                    final.at[chunk, plane],
+                    final.at[chunk, plane],
+                    final_send.at[chunk, step - 1],
+                    final_recv.at[chunk, step - 1],
+                    "dp",
+                    target,
+                )
+            )
+
+    def finish(chunk):
+        for step in range(1, dp_count):
+            final_copies[chunk, step].wait_recv()
+        for part in range(4):
+            weight_out[
+                pl.ds((part // 2) * (shard // 2), shard // 2),
+                pl.ds(chunk * width + (part % 2) * 128, 128),
+            ] = final[chunk, part].astype(jnp.float32) * grad_scale
+
+    forward(0)
+    for copy in halos:
+        copy.wait_recv()
+    for chunk in range(chunks):
+        project(chunk)
+        if chunk + 1 < chunks:
+            forward(chunk + 1)
+        if chunk >= 2:
+            spread(chunk - 2)
+        if chunk >= 1:
+            over_chips(chunk - 1)
+        slopes(chunk)
+        if chunk == chunks - 1:
+            tap_pair = launch(
+                send(tap_own, tap_core, tap_send.at[0], tap_recv.at[0], "seq", sibling)
+            )
+        if chunk >= 1:
+            over_planes(chunk - 1)
+        back(chunk)
+        weight_terms(chunk)
+
+    last = chunks - 1
+    spread(last - 1)
+    tap_pair.wait_recv()
+    tap_chips[chip] = tap_own[...] + tap_core[...]
+    tap_row = []
+    for step in range(1, chips):
+        tap_row.append(
+            launch(
+                send(
+                    tap_chips.at[chip],
+                    tap_chips.at[chip],
+                    tap_send.at[step],
+                    tap_recv.at[step],
+                    "seq",
+                    2 * lax.rem(chip + step, chips) + core,
+                )
+            )
+        )
+    over_chips(last)
+    coarse_grad[...] = jnp.dot(
+        pair_mat[...], grad_merged[...], preferred_element_type=jnp.float32
+    ).astype(jnp.bfloat16)
+    store_coarse = pltpu.make_async_copy(coarse_grad, coarse_out.at[0], local_sem.at[3])
+    store_coarse.start()
+    for copy in tap_row:
+        copy.wait_recv()
+    total = tap_chips[0]
+    for block in range(1, chips):
+        total = total + tap_chips[block]
+    tap_planes[plane] = total
+    tap_line = []
+    for step in range(1, dp_count):
+        tap_line.append(
+            launch(
+                send(
+                    tap_planes.at[plane],
+                    tap_planes.at[plane],
+                    tap_send.at[chips - 1 + step],
+                    tap_recv.at[chips - 1 + step],
+                    "dp",
+                    lax.rem(plane + step, dp_count),
+                )
+            )
+        )
+    over_planes(last)
+    values = jnp.zeros((rows, channels), jnp.float32)
+    for chunk in range(chunks):
+        values = values + lax.dot_general(
+            grad_merged[:, cols(chunk)],
+            weights[chunk].reshape(channels, width),
+            (((1,), (1,)), ((), ())),
+            preferred_element_type=jnp.float32,
+        )
+    skip_grad[...] = values.astype(jnp.bfloat16)
+    store_skip = pltpu.make_async_copy(skip_grad, skip_out.at[0], local_sem.at[4])
+    store_skip.start()
+    for copy in tap_line:
+        copy.wait_recv()
+    total = tap_planes[0]
+    for block in range(1, dp_count):
+        total = total + tap_planes[block]
+    taps_out[...] = total[:3] * grad_scale
+    for chunk in range(last):
+        finish(chunk)
+    spread(last)
+    finish(last)
+    store_coarse.wait()
+    store_skip.wait()
+    for copy in sends:
+        copy.wait_send()
+
+
+def fused(seq_count, dp_count, coarse, skip, skip_weight, depth_taps, cotangent):
+    _, rows, channels = skip.shape
+    shard = skip_weight.shape[0]
+    chunks = channels // width
+    chips = seq_count // 2
+    half, wide = jnp.bfloat16, jnp.float32
+    dma = pltpu.SemaphoreType.DMA
+    extended = rows + 2 * halo
+    return pl.pallas_call(
+        functools.partial(
+            kernel, seq_count, dp_count, 1.0 / math.sqrt(rows * seq_count * dp_count)
+        ),
+        out_shape=(
+            jax.ShapeDtypeStruct(coarse.shape, half),
+            jax.ShapeDtypeStruct(skip.shape, half),
+            jax.ShapeDtypeStruct(skip_weight.shape, wide),
+            jax.ShapeDtypeStruct(depth_taps.shape, wide),
+        ),
+        in_specs=[
+            pl.BlockSpec(memory_space=pl.ANY),
+            pl.BlockSpec(memory_space=pl.ANY),
+            pl.BlockSpec(memory_space=pltpu.VMEM),
+            pl.BlockSpec(memory_space=pltpu.VMEM),
+            pl.BlockSpec(memory_space=pl.ANY),
+        ],
+        out_specs=(
+            pl.BlockSpec(memory_space=pl.ANY),
+            pl.BlockSpec(memory_space=pl.ANY),
+            pl.BlockSpec(memory_space=pltpu.VMEM),
+            pl.BlockSpec(memory_space=pltpu.VMEM),
+        ),
+        scratch_shapes=[
+            pltpu.VMEM((extended, channels), half),
+            pltpu.VMEM((extended, channels), half),
+            pltpu.VMEM((rows // 2 + 2 * halo, channels), half),
+            pltpu.VMEM((channels, rows), half),
+            pltpu.VMEM((extended, rows // 2 + 2 * halo), half),
+            pltpu.VMEM((rows // 2, rows), half),
+            pltpu.VMEM((chunks, seq_count, shard, width), half),
+            pltpu.VMEM((extended, width), wide),
+            pltpu.VMEM((extended, width), wide),
+            pltpu.VMEM((rows, channels), half),
+            pltpu.VMEM((rows // 2, channels), half),
+            pltpu.VMEM((rows, channels), half),
+            pltpu.VMEM((chunks, 2, chips, shard, width), wide),
+            pltpu.VMEM((chunks, 2, chips, shard, width), half),
+            pltpu.VMEM((chunks, chips, shard, width), half),
+            pltpu.VMEM((chunks, chips, shard, width), half),
+            pltpu.VMEM((chunks, shard, width), wide),
+            pltpu.VMEM((chunks, chips - 1, shard, width), half),
+            pltpu.VMEM((chunks, 4, shard // 2, 128), wide),
+            pltpu.VMEM((chunks, 4, shard // 2, 128), half),
+            pltpu.VMEM((chunks, dp_count - 1, shard // 2, 128), half),
+            pltpu.VMEM((chunks, 4, shard // 2, 128), half),
+            pltpu.VMEM((8, channels), wide),
+            pltpu.VMEM((8, channels), wide),
+            pltpu.VMEM((chips, 8, channels), wide),
+            pltpu.VMEM((dp_count, 8, channels), wide),
+            dma((5,)),
+            dma((6,)),
+            dma((6,)),
+            dma((chunks, chips - 1)),
+            dma((chunks, chips - 1)),
+            dma((chunks, chips - 1)),
+            dma((chunks, chips - 1)),
+            dma((chunks,)),
+            dma((chunks,)),
+            dma((chunks,)),
+            dma((chunks,)),
+            dma((chunks, chips - 1)),
+            dma((chunks, chips - 1)),
+            dma((chunks, dp_count - 1)),
+            dma((chunks, dp_count - 1)),
+            dma((chunks, dp_count - 1)),
+            dma((chunks, dp_count - 1)),
+            dma((chips + dp_count - 1,)),
+            dma((chips + dp_count - 1,)),
+        ],
+        compiler_params=pltpu.CompilerParams(
+            collective_id=0, has_side_effects=True, vmem_limit_bytes=48 * 1024 * 1024
+        ),
+    )(coarse, skip, skip_weight, depth_taps, cotangent)
+
+
 def solution(mesh):
     placed = (P("dp", "seq", None), P("dp", "seq", None), P("seq", None), P(), P("dp", "seq", None))
+    seq_count, dp_count = mesh.shape["seq"], mesh.shape["dp"]
+
+    def device_part(coarse, skip, skip_weight, depth_taps, cotangent):
+        fits = (
+            skip.shape[0] == 1
+            and skip.shape[1] % tile == 0
+            and skip.shape[2] % width == 0
+            and skip_weight.shape[0] % 32 == 0
+            and seq_count % 2 == 0
+            and seq_count > 2
+            and dp_count == 4
+        )
+        if fits:
+            return fused(seq_count, dp_count, coarse, skip, skip_weight, depth_taps, cotangent)
+        return local(coarse, skip, skip_weight, depth_taps, cotangent)
+
     return jax.shard_map(
-        local,
+        device_part,
         mesh=mesh,
         in_specs=placed,
         out_specs=(P("dp", "seq", None), P("dp", "seq", None), P("seq", None), P()),

time: 206 us -> 55.1 us (0.27)
  waiting for transfers between devices: 120 us -> 0 us
  Pallas kernels: 0 us -> 46.3 us
  blocking collectives: 43 us -> 0 us
  between operations: 14.2 us -> 0.65 us
  starting transfers between devices: 9.1 us -> 0 us
  other arithmetic: 8.28 us -> 0 us
  matrix products: 6.45 us -> 0 us
  local copies, waits for them, and re-layouts: 4.03 us -> 7.81 us
    psum x1 -> x0, waiting for transfers between devices: 90.4 us -> none  [local(): lax.psum((lax.dot_general(flat_skip, flat_grad, (((0,), (0,)), ((), ())),...]
    pallas_call x0 -> x1, Pallas kernels: none -> 46.3 us  [fused(): pl.pallas_call(functools.partial(kernel, seq_count, dp_count, 1.0 / math....]
    psum x1 -> x0, blocking collectives: 43 us -> none  [local(): lax.psum((lax.dot_general(flat_skip, flat_grad, (((0,), (0,)), ((), ())),...]
    all_gather x1 -> x0, waiting for transfers between devices: 24.9 us -> none  [local(): full_weight = lax.all_gather(skip_weight, 'seq', axis=0, tiled=True)]
    ppermute x4 -> x0, starting transfers between devices: 9.02 us -> none  [the longest x2 6.44 us: padded_2(): lax.ppermute(tail, axis, [(i, (i + 1) % count) for i in range(ends)])]
    unnamed x9 -> x14, local copies, waits for them, and re-layouts: 0.89 us -> 7.81 us
    dot_general x3 -> x0, matrix products: 6.45 us -> none  [the longest x1 2.54 us: local(): jnp.dot(flat_skip, full_weight, preferred_element_type=jnp.float32)]
    reduce_sum x2 -> x0, other arithmetic: 4.66 us -> none  [the longest x1 2.9 us: local(): grad_coarse = grad_merged.astype(jnp.float32).reshape(batch_rows, fine_ro...]
  transfers between devices with their start and end apart: 6 -> 0, of which waited for: 4 -> 0; matrix products, arithmetic and copies ran while one was open for 5% -> 0% of each run, Pallas kernels for 0% -> 0%
where the time goes in v1:
time: 55.1 us; the launch traced here: 54.8 us
  Pallas kernels  46.3 us (84%)
  local copies, waits for them, and re-layouts  7.81 us (14%)
  between operations  0.65 us (1%)
    pallas_call x1, Pallas kernels, fused(): pl.pallas_call(functools.partial(kernel, seq_count, dp_count, 1.0 / math....  46.3 us
    unnamed x14, local copies, waits for them, and re-layouts  7.81 us

profile of v1, /device:TPU:0, one launch (start us, length us, event | category | flops | bytes accessed | tf_op | source)
XLA Modules:
  0.0 54.8 jit_solution(6133632673331031459)
XLA Ops:
  0.6 0.0 copy-start
  0.6 1.1 %copy-done = bf16[1,512,768]{2,1,0:T(8,128)(2,1)S(1)} copy-done((bf16[1,512,768]{2,1,0:T(8,128)(2,1)S(1)}, bf16[1,512,768]{2,1,0:T(8,128)(2,1)}, u32[]{:S(2)}) %copy-start) | copy-done | bytes 786456
  1.8 0.0 copy-start.1
  1.8 1.1 %copy-done.1 = bf16[1,512,768]{2,1,0:T(8,128)(2,1)S(1)} copy-done((bf16[1,512,768]{2,1,0:T(8,128)(2,1)S(1)}, bf16[1,512,768]{2,1,0:T(8,128)(2,1)}, u32[]{:S(2)}) %copy-start.1) | copy-done | bytes 786456
  2.9 0.0 copy-start.2
  2.9 1.0 %copy-done.2 = bf16[1,256,768]{2,1,0:T(8,128)(2,1)S(1)} copy-done((bf16[1,256,768]{2,1,0:T(8,128)(2,1)S(1)}, bf16[1,256,768]{2,1,0:T(8,128)(2,1)}, u32[]{:S(2)}) %copy-start.2) | copy-done | bytes 393240
  3.9 0.0 copy-start.3
  3.9 0.9 %copy-done.3 = bf16[96,768]{1,0:T(8,128)(2,1)S(1)} copy-done((bf16[96,768]{1,0:T(8,128)(2,1)S(1)}, bf16[96,768]{1,0:T(8,128)(2,1)}, u32[]{:S(2)}) %copy-start.3) | copy-done | bytes 147480
  4.8 0.0 copy-start.4
  4.8 0.7 %copy-done.4 = f32[3,768]{1,0:T(4,128)S(1)} copy-done((f32[3,768]{1,0:T(4,128)S(1)}, f32[3,768]{1,0:T(4,128)}, u32[]{:S(2)}) %copy-start.4) | copy-done | bytes 9240
  5.5 46.3 %shard_map.84 = (bf16[1,256,768]{2,1,0:T(8,128)(2,1)S(1)}, bf16[1,512,768]{2,1,0:T(8,128)(2,1)S(1)}, f32[96,768]{1,0:T(8,128)S(1)}, f32[3,768]{1,0:T(4,128)S(1)}) custom-call(bf16[1,256,768]{2,1,0:T(8,128)(2,1)S(1)} %copy-done.2, bf16[1,512,768]{2,1,0:T(8,128)(2,1)S(1)} %copy-done, bf16[96,768]{1,0:T(8,128)(2,1)S(1)} %copy-done.3, f32[3,768]{1,0:T(4,128)S(1)} %copy-done.4, ...), custom_call_target="tpu_custom_call" | custom-call | tf_op jit(solution)/shard_map/pallas_call | solution.py:565
  51.8 0.7 %copy.13 = bf16[1,256,768]{2,1,0:T(8,128)(2,1)} copy(bf16[1,256,768]{2,1,0:T(8,128)(2,1)S(1)} %get-tuple-element.8) | data formatting | bytes 786432
  52.6 0.9 %copy.14 = bf16[1,512,768]{2,1,0:T(8,128)(2,1)} copy(bf16[1,512,768]{2,1,0:T(8,128)(2,1)S(1)} %get-tuple-element.9) | data formatting | bytes 1572864
  53.4 0.7 %copy.15 = f32[96,768]{1,0:T(8,128)} copy(f32[96,768]{1,0:T(8,128)S(1)} %get-tuple-element.10) | data formatting | bytes 589824
  54.2 0.6 %copy.16 = f32[3,768]{1,0:T(4,128)} copy(f32[3,768]{1,0:T(4,128)S(1)} %get-tuple-element.11) | data formatting | bytes 18432
Async XLA Ops:
  0.6 1.1 %copy-start = (bf16[1,512,768]{2,1,0:T(8,128)(2,1)S(1)}, bf16[1,512,768]{2,1,0:T(8,128)(2,1)}, u32[]{:S(2)}) copy-start(bf16[1,512,768]{2,1,0:T(8,128)(2,1)} %skip_hbm.1) | copy-start | bytes 2359300
  1.8 1.1 %copy-start.1 = (bf16[1,512,768]{2,1,0:T(8,128)(2,1)S(1)}, bf16[1,512,768]{2,1,0:T(8,128)(2,1)}, u32[]{:S(2)}) copy-start(bf16[1,512,768]{2,1,0:T(8,128)(2,1)} %cot_hbm.1) | copy-start | bytes 2359300
  2.9 1.0 %copy-start.2 = (bf16[1,256,768]{2,1,0:T(8,128)(2,1)S(1)}, bf16[1,256,768]{2,1,0:T(8,128)(2,1)}, u32[]{:S(2)}) copy-start(bf16[1,256,768]{2,1,0:T(8,128)(2,1)} %coarse_hbm.1) | copy-start | bytes 1179652
  3.9 0.9 %copy-start.3 = (bf16[96,768]{1,0:T(8,128)(2,1)S(1)}, bf16[96,768]{1,0:T(8,128)(2,1)}, u32[]{:S(2)}) copy-start(bf16[96,768]{1,0:T(8,128)(2,1)} %weight_ref.1) | copy-start | bytes 442372
  4.8 0.7 %copy-start.4 = (f32[3,768]{1,0:T(4,128)S(1)}, f32[3,768]{1,0:T(4,128)}, u32[]{:S(2)}) copy-start(f32[3,768]{1,0:T(4,128)} %taps_ref.1) | copy-start | bytes 27652

commit v2 on v1

--- a/solution.py
+++ b/solution.py
@@ -121,9 +121,13 @@
     grad_scale,
     coarse_hbm,
     skip_hbm,
-    weight_ref,
-    taps_ref,
+    weight_hbm,
+    taps_hbm,
     cot_hbm,
+    coarse_hbm_out,
+    skip_hbm_out,
+    weight_hbm_out,
+    taps_hbm_out,
     coarse_out,
     skip_out,
     weight_out,
@@ -138,8 +142,6 @@
     merged,
     grad_pre,
     grad_merged,
-    coarse_grad,
-    skip_grad,
     term_wide,
     term_half,
     from_core,
@@ -150,6 +152,7 @@
     plane_half,
     from_planes,
     final,
+    taps_ref,
     tap_own,
     tap_core,
     tap_chips,
@@ -176,7 +179,7 @@
 ):
     rows = skip_hbm.shape[1]
     channels = skip_hbm.shape[2]
-    shard = weight_ref.shape[0]
+    shard = weight_hbm.shape[0]
     chunks = channels // width
     chips = seq_count // 2
     me = lax.axis_index("seq")
@@ -194,6 +197,15 @@
             coarse_hbm.at[0], coarse_ext.at[pl.ds(halo, rows // 2)], local_sem.at[2]
         ),
     ]
+    loads.append(pltpu.make_async_copy(taps_hbm, taps_ref, local_sem.at[3]))
+    for chunk in range(channels // width):
+        loads.append(
+            pltpu.make_async_copy(
+                weight_hbm.at[:, pl.ds(chunk * width, width)],
+                weights.at[chunk, me],
+                local_sem.at[4 + chunk],
+            )
+        )
     for copy in loads:
         copy.start()
 
@@ -209,6 +221,14 @@
     pl.semaphore_wait(barrier, seq_count + dp_count - 2)
 
     sends = []
+    stores = []
+
+    def write(source, target, number):
+        stores.append(
+            pltpu.make_async_copy(source, target, local_sem.at[4 + channels // width + number])
+        )
+        stores[-1].start()
+
 
     def launch(copy):
         copy.start()
@@ -225,7 +245,7 @@
             target = 2 * lax.rem(chip + step, chips) + core
             gathers[chunk, step] = launch(
                 send(
-                    weight_ref.at[:, cols(chunk)],
+                    weight_hbm.at[:, cols(chunk)],
                     weights.at[chunk, me],
                     gather_send.at[chunk, step - 1],
                     gather_recv.at[chunk, step - 1],
@@ -235,7 +255,7 @@
             )
         own_halves[chunk] = launch(
             send(
-                weight_ref.at[:, cols(chunk)],
+                weight_hbm.at[:, cols(chunk)],
                 weights.at[chunk, me],
                 sib_send.at[chunk],
                 sib_recv.at[chunk],
@@ -275,8 +295,6 @@
     for chunk in range(1, chunks):
         gather(chunk)
 
-    for chunk in range(chunks):
-        weights[chunk, me] = weight_ref[:, cols(chunk)]
     out_row = lax.broadcasted_iota(jnp.int32, repeat_mat.shape, 0)
     in_row = lax.broadcasted_iota(jnp.int32, repeat_mat.shape, 1)
     repeat_mat[...] = jnp.where(
@@ -461,29 +479,30 @@
                 pl.ds(chunk * width + (part % 2) * 128, 128),
             ] = final[chunk, part].astype(jnp.float32) * grad_scale
 
+    last = chunks - 1
     forward(0)
     for copy in halos:
         copy.wait_recv()
     for chunk in range(chunks):
         project(chunk)
-        if chunk + 1 < chunks:
-            forward(chunk + 1)
-        if chunk >= 2:
-            spread(chunk - 2)
         if chunk >= 1:
             over_chips(chunk - 1)
+        if chunk >= 2:
+            over_planes(chunk - 2)
         slopes(chunk)
-        if chunk == chunks - 1:
+        if chunk < last:
+            forward(chunk + 1)
+        else:
             tap_pair = launch(
                 send(tap_own, tap_core, tap_send.at[0], tap_recv.at[0], "seq", sibling)
             )
-        if chunk >= 1:
-            over_planes(chunk - 1)
         back(chunk)
         weight_terms(chunk)
 
-    last = chunks - 1
-    spread(last - 1)
+    for chunk in range(last - 1):
+        spread(chunk)
+    over_chips(last)
+    over_planes(last - 1)
     tap_pair.wait_recv()
     tap_chips[chip] = tap_own[...] + tap_core[...]
     tap_row = []
@@ -500,12 +519,20 @@
                 )
             )
         )
-    over_chips(last)
-    coarse_grad[...] = jnp.dot(
+    values = jnp.zeros((rows, channels), jnp.float32)
+    for chunk in range(chunks):
+        values = values + lax.dot_general(
+            grad_merged[:, cols(chunk)],
+            weights[chunk].reshape(channels, width),
+            (((1,), (1,)), ((), ())),
+            preferred_element_type=jnp.float32,
+        )
+    skip_out[0] = values.astype(jnp.bfloat16)
+    write(skip_out, skip_hbm_out, 0)
+    coarse_out[0] = jnp.dot(
         pair_mat[...], grad_merged[...], preferred_element_type=jnp.float32
     ).astype(jnp.bfloat16)
-    store_coarse = pltpu.make_async_copy(coarse_grad, coarse_out.at[0], local_sem.at[3])
-    store_coarse.start()
+    write(coarse_out, coarse_hbm_out, 1)
     for copy in tap_row:
         copy.wait_recv()
     total = tap_chips[0]
@@ -527,31 +554,36 @@
             )
         )
     over_planes(last)
-    values = jnp.zeros((rows, channels), jnp.float32)
-    for chunk in range(chunks):
-        values = values + lax.dot_general(
-            grad_merged[:, cols(chunk)],
-            weights[chunk].reshape(channels, width),
-            (((1,), (1,)), ((), ())),
-            preferred_element_type=jnp.float32,
-        )
-    skip_grad[...] = values.astype(jnp.bfloat16)
-    store_skip = pltpu.make_async_copy(skip_grad, skip_out.at[0], local_sem.at[4])
-    store_skip.start()
+    spread(last - 1)
     for copy in tap_line:
         copy.wait_recv()
     total = tap_planes[0]
     for block in range(1, dp_count):
         total = total + tap_planes[block]
     taps_out[...] = total[:3] * grad_scale
-    for chunk in range(last):
+    write(taps_out, taps_hbm_out, 2)
+    for chunk in range(last - 1):
         finish(chunk)
     spread(last)
+    finish(last - 1)
     finish(last)
-    store_coarse.wait()
-    store_skip.wait()
+    write(weight_out, weight_hbm_out, 3)
+    for copy in stores:
+        copy.wait()
     for copy in sends:
         copy.wait_send()
+
+
+def store(*refs):
+    loads = [pltpu.make_async_copy(refs[k], refs[8 + k], refs[12].at[k]) for k in range(4)]
+    writes = [pltpu.make_async_copy(refs[8 + k], refs[4 + k], refs[13].at[k]) for k in range(4)]
+    for copy in loads:
+        copy.start()
+    for load, write in zip(loads, writes):
+        load.wait()
+        write.start()
+    for copy in writes:
+        copy.wait()
 
 
 def fused(seq_count, dp_count, coarse, skip, skip_weight, depth_taps, cotangent):
@@ -562,7 +594,7 @@
     half, wide = jnp.bfloat16, jnp.float32
     dma = pltpu.SemaphoreType.DMA
     extended = rows + 2 * halo
-    return pl.pallas_call(
+    results = pl.pallas_call(
         functools.partial(
             kernel, seq_count, dp_count, 1.0 / math.sqrt(rows * seq_count * dp_count)
         ),
@@ -572,20 +604,13 @@
             jax.ShapeDtypeStruct(skip_weight.shape, wide),
             jax.ShapeDtypeStruct(depth_taps.shape, wide),
         ),
-        in_specs=[
-            pl.BlockSpec(memory_space=pl.ANY),
-            pl.BlockSpec(memory_space=pl.ANY),
-            pl.BlockSpec(memory_space=pltpu.VMEM),
-            pl.BlockSpec(memory_space=pltpu.VMEM),
-            pl.BlockSpec(memory_space=pl.ANY),
-        ],
-        out_specs=(
-            pl.BlockSpec(memory_space=pl.ANY),
-            pl.BlockSpec(memory_space=pl.ANY),
-            pl.BlockSpec(memory_space=pltpu.VMEM),
-            pl.BlockSpec(memory_space=pltpu.VMEM),
-        ),
+        in_specs=[pl.BlockSpec(memory_space=pltpu.HBM)] * 5,
+        out_specs=(pl.BlockSpec(memory_space=pltpu.HBM),) * 4,
         scratch_shapes=[
+            pltpu.VMEM(coarse.shape, half),
+            pltpu.VMEM(skip.shape, half),
+            pltpu.VMEM(skip_weight.shape, wide),
+            pltpu.VMEM(depth_taps.shape, wide),
             pltpu.VMEM((extended, channels), half),
             pltpu.VMEM((extended, channels), half),
             pltpu.VMEM((rows // 2 + 2 * halo, channels), half),
@@ -595,8 +620,6 @@
             pltpu.VMEM((chunks, seq_count, shard, width), half),
             pltpu.VMEM((extended, width), wide),
             pltpu.VMEM((extended, width), wide),
-            pltpu.VMEM((rows, channels), half),
-            pltpu.VMEM((rows // 2, channels), half),
             pltpu.VMEM((rows, channels), half),
             pltpu.VMEM((chunks, 2, chips, shard, width), wide),
             pltpu.VMEM((chunks, 2, chips, shard, width), half),
@@ -608,11 +631,12 @@
             pltpu.VMEM((chunks, 4, shard // 2, 128), half),
             pltpu.VMEM((chunks, dp_count - 1, shard // 2, 128), half),
             pltpu.VMEM((chunks, 4, shard // 2, 128), half),
+            pltpu.VMEM(depth_taps.shape, wide),
             pltpu.VMEM((8, channels), wide),
             pltpu.VMEM((8, channels), wide),
             pltpu.VMEM((chips, 8, channels), wide),
             pltpu.VMEM((dp_count, 8, channels), wide),
-            dma((5,)),
+            dma((8 + chunks,)),
             dma((6,)),
             dma((6,)),
             dma((chunks, chips - 1)),
@@ -633,9 +657,18 @@
             dma((chips + dp_count - 1,)),
         ],
         compiler_params=pltpu.CompilerParams(
-            collective_id=0, has_side_effects=True, vmem_limit_bytes=48 * 1024 * 1024
+            collective_id=0, has_side_effects=True, vmem_limit_bytes=62 * 1024 * 1024
         ),
     )(coarse, skip, skip_weight, depth_taps, cotangent)
+    return pl.pallas_call(
+        store,
+        out_shape=tuple(jax.ShapeDtypeStruct(part.shape, part.dtype) for part in results),
+        in_specs=[pl.BlockSpec(memory_space=pltpu.HBM)] * 4,
+        out_specs=(pl.BlockSpec(memory_space=pltpu.HBM),) * 4,
+        scratch_shapes=[pltpu.VMEM(part.shape, part.dtype) for part in results]
+        + [dma((4,)), dma((4,))],
+        compiler_params=pltpu.CompilerParams(vmem_limit_bytes=62 * 1024 * 1024),
+    )(*results)
 
 
 def solution(mesh):

time: 55.1 us -> 43.7 us (0.79)
  local copies, waits for them, and re-layouts: 7.81 us -> 0 us
  Pallas kernels: 46.3 us -> 42.9 us
    unnamed x14 -> x0, local copies, waits for them, and re-layouts: 7.81 us -> none
    pallas_call x1, Pallas kernels: 46.3 us -> 40.6 us  [fused(): pl.pallas_call(functools.partial(kernel, seq_count, dp_count, 1.0 / math....]
    pallas_call x0 -> x1, Pallas kernels: none -> 2.3 us  [fused(): pl.pallas_call(store, out_shape=tuple((jax.ShapeDtypeStruct(part.shape, p...]
where the time goes in v2:
time: 43.7 us; the launch traced here: 43.6 us
  Pallas kernels  42.9 us (98%)
  between operations  0.64 us (1%)
    pallas_call x1, Pallas kernels, fused(): pl.pallas_call(functools.partial(kernel, seq_count, dp_count, 1.0 / math....  40.6 us
    pallas_call x1, Pallas kernels, fused(): pl.pallas_call(store, out_shape=tuple((jax.ShapeDtypeStruct(part.shape, p...  2.3 us

profile of v2, /device:TPU:0, one launch (start us, length us, event | category | flops | bytes accessed | tf_op | source)
XLA Modules:
  0.0 43.6 jit_solution(16254885559844261876)
XLA Ops:
  0.6 40.6 %shard_map.84 = (bf16[1,256,768]{2,1,0:T(8,128)(2,1)}, bf16[1,512,768]{2,1,0:T(8,128)(2,1)}, f32[96,768]{1,0:T(8,128)}, f32[3,768]{1,0:T(4,128)}) custom-call(bf16[1,256,768]{2,1,0:T(8,128)(2,1)} %coarse_hbm.1, bf16[1,512,768]{2,1,0:T(8,128)(2,1)} %skip_hbm.1, bf16[96,768]{1,0:T(8,128)(2,1)} %weight_hbm.1, f32[3,768]{1,0:T(4,128)} %taps_hbm.1, ...), custom_call_target="tpu_custom_call" | custom-call | tf_op jit(solution)/shard_map/pallas_call | solution.py:597
  41.3 2.3 %shard_map.85 = (bf16[1,256,768]{2,1,0:T(8,128)(2,1)}, bf16[1,512,768]{2,1,0:T(8,128)(2,1)}, f32[96,768]{1,0:T(8,128)}, f32[3,768]{1,0:T(4,128)}) custom-call(bf16[1,256,768]{2,1,0:T(8,128)(2,1)} %get-tuple-element.8.refs_0_, bf16[1,512,768]{2,1,0:T(8,128)(2,1)} %get-tuple-element.9.refs_1_, f32[96,768]{1,0:T(8,128)} %get-tuple-element.10.refs_2_, ...), custom_call_target="tpu_custom_call" | custom-call | tf_op jit(solution)/shard_map/pallas_call | solution.py:663

commit v3 on v2

--- a/solution.py
+++ b/solution.py
@@ -499,8 +499,6 @@
         back(chunk)
         weight_terms(chunk)
 
-    for chunk in range(last - 1):
-        spread(chunk)
     over_chips(last)
     over_planes(last - 1)
     tap_pair.wait_recv()
@@ -519,6 +517,8 @@
                 )
             )
         )
+    for chunk in range(last - 1):
+        spread(chunk)
     values = jnp.zeros((rows, channels), jnp.float32)
     for chunk in range(chunks):
         values = values + lax.dot_general(
@@ -533,6 +533,7 @@
         pair_mat[...], grad_merged[...], preferred_element_type=jnp.float32
     ).astype(jnp.bfloat16)
     write(coarse_out, coarse_hbm_out, 1)
+    over_planes(last)
     for copy in tap_row:
         copy.wait_recv()
     total = tap_chips[0]
@@ -553,8 +554,11 @@
                 )
             )
         )
-    over_planes(last)
     spread(last - 1)
+    for chunk in range(last - 1):
+        finish(chunk)
+    spread(last)
+    finish(last - 1)
     for copy in tap_line:
         copy.wait_recv()
     total = tap_planes[0]
@@ -562,10 +566,6 @@
         total = total + tap_planes[block]
     taps_out[...] = total[:3] * grad_scale
     write(taps_out, taps_hbm_out, 2)
-    for chunk in range(last - 1):
-        finish(chunk)
-    spread(last)
-    finish(last - 1)
     finish(last)
     write(weight_out, weight_hbm_out, 3)
     for copy in stores:

time: 43.7 us -> 41.4 us (0.947)
  Pallas kernels: 42.9 us -> 40.6 us
    pallas_call x1, Pallas kernels: 40.6 us -> 38.3 us  [fused(): pl.pallas_call(functools.partial(kernel, seq_count, dp_count, 1.0 / math....]
where the time goes in v3:
time: 41.4 us; the launch traced here: 41.2 us
  Pallas kernels  40.6 us (98%)
  between operations  0.64 us (2%)
    pallas_call x1, Pallas kernels, fused(): pl.pallas_call(functools.partial(kernel, seq_count, dp_count, 1.0 / math....  38.3 us
    pallas_call x1, Pallas kernels, fused(): pl.pallas_call(store, out_shape=tuple((jax.ShapeDtypeStruct(part.shape, p...  2.3 us

profile of v3, /device:TPU:0, one launch (start us, length us, event | category | flops | bytes accessed | tf_op | source)
XLA Modules:
  0.0 41.2 jit_solution(637248099395418011)
XLA Ops:
  0.6 38.3 %shard_map.84 = (bf16[1,256,768]{2,1,0:T(8,128)(2,1)}, bf16[1,512,768]{2,1,0:T(8,128)(2,1)}, f32[96,768]{1,0:T(8,128)}, f32[3,768]{1,0:T(4,128)}) custom-call(bf16[1,256,768]{2,1,0:T(8,128)(2,1)} %coarse_hbm.1, bf16[1,512,768]{2,1,0:T(8,128)(2,1)} %skip_hbm.1, bf16[96,768]{1,0:T(8,128)(2,1)} %weight_hbm.1, f32[3,768]{1,0:T(4,128)} %taps_hbm.1, ...), custom_call_target="tpu_custom_call" | custom-call | tf_op jit(solution)/shard_map/pallas_call | solution.py:597
  38.9 2.3 %shard_map.85 = (bf16[1,256,768]{2,1,0:T(8,128)(2,1)}, bf16[1,512,768]{2,1,0:T(8,128)(2,1)}, f32[96,768]{1,0:T(8,128)}, f32[3,768]{1,0:T(4,128)}) custom-call(bf16[1,256,768]{2,1,0:T(8,128)(2,1)} %get-tuple-element.8.refs_0_, bf16[1,512,768]{2,1,0:T(8,128)(2,1)} %get-tuple-element.9.refs_1_, f32[96,768]{1,0:T(8,128)} %get-tuple-element.10.refs_2_, ...), custom_call_target="tpu_custom_call" | custom-call | tf_op jit(solution)/shard_map/pallas_call | solution.py:663

commit v4 on v3

--- a/solution.py
+++ b/solution.py
@@ -487,9 +487,9 @@
         project(chunk)
         if chunk >= 1:
             over_chips(chunk - 1)
+        slopes(chunk)
         if chunk >= 2:
             over_planes(chunk - 2)
-        slopes(chunk)
         if chunk < last:
             forward(chunk + 1)
         else:

time: 41.4 us -> 40.6 us (0.981)
  Pallas kernels: 40.6 us -> 39.8 us
    pallas_call x1, Pallas kernels: 38.3 us -> 37.5 us  [fused(): pl.pallas_call(functools.partial(kernel, seq_count, dp_count, 1.0 / math....]
where the time goes in v4:
time: 40.6 us; the launch traced here: 40.5 us
  Pallas kernels  39.8 us (98%)
  between operations  0.64 us (2%)
    pallas_call x1, Pallas kernels, fused(): pl.pallas_call(functools.partial(kernel, seq_count, dp_count, 1.0 / math....  37.5 us
    pallas_call x1, Pallas kernels, fused(): pl.pallas_call(store, out_shape=tuple((jax.ShapeDtypeStruct(part.shape, p...  2.3 us

profile of v4, /device:TPU:0, one launch (start us, length us, event | category | flops | bytes accessed | tf_op | source)
XLA Modules:
  0.0 40.5 jit_solution(8091370195171875915)
XLA Ops:
  0.6 37.5 %shard_map.84 = (bf16[1,256,768]{2,1,0:T(8,128)(2,1)}, bf16[1,512,768]{2,1,0:T(8,128)(2,1)}, f32[96,768]{1,0:T(8,128)}, f32[3,768]{1,0:T(4,128)}) custom-call(bf16[1,256,768]{2,1,0:T(8,128)(2,1)} %coarse_hbm.1, bf16[1,512,768]{2,1,0:T(8,128)(2,1)} %skip_hbm.1, bf16[96,768]{1,0:T(8,128)(2,1)} %weight_hbm.1, f32[3,768]{1,0:T(4,128)} %taps_hbm.1, ...), custom_call_target="tpu_custom_call" | custom-call | tf_op jit(solution)/shard_map/pallas_call | solution.py:597
  38.2 2.3 %shard_map.85 = (bf16[1,256,768]{2,1,0:T(8,128)(2,1)}, bf16[1,512,768]{2,1,0:T(8,128)(2,1)}, f32[96,768]{1,0:T(8,128)}, f32[3,768]{1,0:T(4,128)}) custom-call(bf16[1,256,768]{2,1,0:T(8,128)(2,1)} %get-tuple-element.8.refs_0_, bf16[1,512,768]{2,1,0:T(8,128)(2,1)} %get-tuple-element.9.refs_1_, f32[96,768]{1,0:T(8,128)} %get-tuple-element.10.refs_2_, ...), custom_call_target="tpu_custom_call" | custom-call | tf_op jit(solution)/shard_map/pallas_call | solution.py:663
